TPU v7x, 256 devices: a whole 4x4x8 slice. The times are simulated.
256 devices in a mesh: row: 32 (over y, z), col: 2 (over core), depth: 4 (over x).
Axes of the slice: x: 4, y: 4, z: 8, core: 2. Of those that a mesh axis runs over, the one named last changes fastest.
Arguments:
- lower_prev: float32 [3, 1024, 4096], P(None, 'row', 'depth'), may hold values from -0.09375 to 0.09375
- inner_blocks: float32 [3, 1024, 1024], P(None, 'row', 'depth'), may hold values from -0.1875 to 0.1875
- diag_inverse: float32 [3, 1024, 1024], P(None, 'depth'), as said below
- known_rows: float32 [4096, 2048], P('depth', 'col'), may hold values from -6 to 6
- right_sides: float32 [3, 1024, 2048], P(None, 'row', 'col'), may hold values from -6 to 6
Outputs:
- solved: float32 [3, 1024, 2048], P(None, 'depth', 'col')
Inputs may be any that keep to these rules, and one draw needn't show every extreme that they name: Each diag_inverse[k] is lower triangular with diagonal entries between 0.7 and 1.3; its entries below the diagonal are of order 0.02 (normal with spread 0.6/32).
All inputs are finite; a program needn't handle non-finite values.
Results may differ from a plain program's by a relative error of at most 0.0001.
Values sent between devices are 32-bit elements; how exact they have to be, the bound alone decides.
A program may use at most 64 MiB of HBM per device.

v0:
```python
import jax
import jax.numpy as jnp
from jax import lax
from jax.sharding import PartitionSpec as P


def on_device(lower_prev, inner_blocks, diag_inverse, known_rows, right_sides):
    highest = lax.Precision.HIGHEST
    row_count = lower_prev.shape[1]
    row_index = lax.axis_index("row")
    earlier_map = [[], [(0, 0)], [(0, 1), (1, 2)]]
    flattened = lower_prev.reshape(3 * row_count, lower_prev.shape[2])
    prev_all = jnp.dot(flattened, known_rows, precision=highest, preferred_element_type=jnp.float32)
    prev_terms = [prev_all[section * row_count : (section + 1) * row_count] for section in range(3)]
    solved = []
    for section in range(3):
        update = prev_terms[section]
        for earlier, which in earlier_map[section]:
            update = update + jnp.dot(
                inner_blocks[which],
                solved[earlier],
                precision=highest,
                preferred_element_type=jnp.float32,
            )
        summed = lax.psum(update, "depth")
        reduced = right_sides[section] - summed
        inverse_rows = diag_inverse[section]
        columns = lax.dynamic_slice_in_dim(inverse_rows, row_index * row_count, row_count, 1)
        partial_sum = jnp.dot(
            columns, reduced, precision=highest, preferred_element_type=jnp.float32
        )
        solution = lax.psum(partial_sum, "row")
        solved.append(solution)
    return jnp.stack(solved)


def solution(mesh):
    placed = (
        P(None, "row", "depth"),
        P(None, "row", "depth"),
        P(None, "depth", None),
        P("depth", "col"),
        P(None, "row", "col"),
    )
    return jax.shard_map(
        on_device, mesh=mesh, in_specs=placed, out_specs=P(None, "depth", "col"), check_vma=False
    )
```

profile of v0, /device:TPU:2, one launch (start us, length us, event | category | flops | bytes accessed | tf_op | source)
XLA Modules:
  0.0 626.3 jit_solution(8888036773343827988)
XLA Ops:
  6.5 0.0 copy-start
  6.5 0.0 all-reduce.7.cloned.1.call-start
  6.5 1.0 copy-done
  7.5 4.7 fusion.24
  12.3 0.7 slice.48
  12.9 0.0 all-reduce.7.cloned.1.call-update
  12.9 0.0 copy-start.3
  13.0 0.0 copy-start.4
  13.0 0.0 all-reduce.9.cloned.1.call-start
  13.0 3.2 fusion.23
  16.2 44.9 %all-reduce.7.cloned.1.call-done = f32[32,1024]{1,0:T(8,128)} async-done(((f32[32,1024]{1,0:T(8,128)}), f32[32,1024]{1,0:T(8,128)}) %all-reduce.7.cloned.1.call-update) | async-done | bytes 131088 | tf_op jit(solution)/shard_map/psum | solution.py:25
  61.2 0.0 copy-done.3
  61.2 3.0 fusion.6
  64.2 0.0 all-reduce.9.cloned.1.call-update
  64.2 0.0 all-reduce.11.cloned.1.call-start
  64.2 151.9 %all-reduce.9.cloned.1.call-done = f32[256,1024]{1,0:T(8,128)} async-done(((f32[256,1024]{1,0:T(8,128)}), f32[256,1024]{1,0:T(8,128)}) %all-reduce.9.cloned.1.call-update) | async-done | bytes 1048592 | tf_op jit(solution)/shard_map/psum | solution.py:32
  216.2 0.0 copy-done.4
  216.2 0.0 copy-start.1
  216.2 2.7 fusion
  218.9 0.0 all-reduce.11.cloned.1.call-update
  218.9 0.0 all-reduce.13.cloned.1.call-start
  218.9 42.6 %all-reduce.11.cloned.1.call-done = f32[32,1024]{1,0:T(8,128)} async-done(((f32[32,1024]{1,0:T(8,128)}), f32[32,1024]{1,0:T(8,128)}) %all-reduce.11.cloned.1.call-update) | async-done | bytes 131088 | tf_op jit(solution)/shard_map/psum | solution.py:25
  261.5 3.0 fusion.4
  264.5 0.0 all-reduce.13.cloned.1.call-update
  264.6 0.0 all-reduce.15.cloned.1.call-start
  264.6 0.0 copy-done.1
  264.6 1.4 fusion.1
  266.0 150.0 %all-reduce.13.cloned.1.call-done = f32[256,1024]{1,0:T(8,128)} async-done(((f32[256,1024]{1,0:T(8,128)}), f32[256,1024]{1,0:T(8,128)}) %all-reduce.13.cloned.1.call-update) | async-done | bytes 1048592 | tf_op jit(solution)/shard_map/psum | solution.py:32
  416.0 0.0 copy-start.2
  416.0 2.7 fusion.2
  418.7 0.0 all-reduce.15.cloned.1.call-update
  418.8 0.0 all-reduce.17.cloned.1.call-start
  418.8 42.6 %all-reduce.15.cloned.1.call-done = f32[32,1024]{1,0:T(8,128)} async-done(((f32[32,1024]{1,0:T(8,128)}), f32[32,1024]{1,0:T(8,128)}) %all-reduce.15.cloned.1.call-update) | async-done | bytes 131088 | tf_op jit(solution)/shard_map/psum | solution.py:25
  461.4 3.0 convolution_bitcast_fusion
  464.4 0.0 all-reduce.17.cloned.1.call-update
  464.4 151.8 %all-reduce.17.cloned.1.call-done = f32[1,256,1024]{2,1,0:T(8,128)} async-done(((f32[1,256,1024]{2,1,0:T(8,128)}), f32[1,256,1024]{2,1,0:T(8,128)}) %all-reduce.17.cloned.1.call-update) | async-done | bytes 1048592 | tf_op jit(solution)/shard_map/psum | solution.py:32
  616.2 0.0 copy-done.2
  616.2 3.2 pad_maximum_fusion
Async XLA Ops:
  6.5 1.0 copy-start
  6.5 54.6 %all-reduce.7.cloned.1.call-start = ((), (), s32[]{:S(2)}) async-start(), calls=%async_computation | async-start | bytes 262144 | tf_op jit(solution)/shard_map/psum | solution.py:25
  12.9 48.2 %copy-start.3 = (f32[3,32,1024]{2,1,0:T(8,128)S(1)}, f32[3,32,1024]{2,1,0:T(8,128)}, u32[]{:S(2)}) copy-start(f32[3,32,1024]{2,1,0:T(8,128)} %param.9) | copy-start | bytes 1179652
  13.0 203.2 %copy-start.4 = (f32[3,32,256]{2,1,0:T(8,128)S(1)}, f32[3,32,256]{2,1,0:T(8,128)}, u32[]{:S(2)}) copy-start(f32[3,32,256]{2,1,0:T(8,128)} %param.6) | copy-start | bytes 294916
  13.0 203.2 %all-reduce.9.cloned.1.call-start = ((), (), s32[]{:S(2)}) async-start(), calls=%async_computation.1 | async-start | bytes 2097152 | tf_op jit(solution)/shard_map/psum | solution.py:32
  64.2 197.4 %all-reduce.11.cloned.1.call-start = ((), (), s32[]{:S(2)}) async-start(), calls=%async_computation.2 | async-start | bytes 262144 | tf_op jit(solution)/shard_map/psum | solution.py:25
  216.2 48.4 %copy-start.1 = (f32[256,1024]{1,0:T(8,128)S(1)}, f32[256,1024]{1,0:T(8,128)}, u32[]{:S(2)}) copy-start(f32[256,1024]{1,0:T(8,128)} %all-reduce.9.cloned.1.call-done) | copy-start | bytes 3145732
  218.9 197.1 %all-reduce.13.cloned.1.call-start = ((), (), s32[]{:S(2)}) async-start(), calls=%async_computation.3 | async-start | bytes 2097152 | tf_op jit(solution)/shard_map/psum | solution.py:32
  264.6 196.8 %all-reduce.15.cloned.1.call-start = ((), (), s32[]{:S(2)}) async-start(), calls=%async_computation.4 | async-start | bytes 262144 | tf_op jit(solution)/shard_map/psum | solution.py:25
  416.0 200.2 %copy-start.2 = (f32[256,1024]{1,0:T(8,128)S(1)}, f32[256,1024]{1,0:T(8,128)}, u32[]{:S(2)}) copy-start(f32[256,1024]{1,0:T(8,128)} %all-reduce.13.cloned.1.call-done) | copy-start | bytes 3145732
  418.8 197.5 %all-reduce.17.cloned.1.call-start = ((), (), s32[]{:S(2)}) async-start(), calls=%async_computation.5 | async-start | bytes 2097152 | tf_op jit(solution)/shard_map/psum | solution.py:32
Sparse Core Ops, SparseCore 0:
  13.1 48.0 all-reduce.6
  65.0 151.1 all-reduce.8
  219.0 42.4 all-reduce.10
  264.8 151.1 all-reduce.12
  418.9 42.4 all-reduce.14
  465.1 151.0 all-reduce.16
where the time goes:
time: 627 us; the launch traced here: 626 us
  waiting for transfers between devices  584 us (93%)
  matrix products  20.5 us (3%)
  between operations  13.5 us (2%)
    psum x3, waiting for transfers between devices, on_device(): solution = lax.psum(partial_sum, 'row')  454 us
    psum x3, waiting for transfers between devices, on_device(): summed = lax.psum(update, 'depth')  130 us
  transfers between devices with their start and end apart: 6, of which 6 were waited for; matrix products, arithmetic and copies ran while one was open for 1% of the time, Pallas kernels for 0%

commit v1 on v0

v1 whole, which is shorter than its diff:
```python
import functools

import jax
import jax.numpy as jnp
from jax import lax
from jax.experimental import pallas as pl
from jax.experimental.pallas import tpu as pltpu
from jax.sharding import PartitionSpec as P

MESH = pl.DeviceIdType.MESH
T = 8
LANES = 128


def split(value):
    high = value.astype(jnp.bfloat16)
    low = (value - high.astype(jnp.float32)).astype(jnp.bfloat16)
    return high, low


def dot(a, b):
    return jnp.dot(a, b, preferred_element_type=jnp.float32)


def three_pass(a_high, a_low, b):
    b_high, b_low = split(b)
    width = b.shape[1]
    both = dot(a_high, jnp.concatenate([b_high, b_low], axis=1))
    return both[:, :width] + (both[:, width:] + dot(a_low, b_high))


def wait_bytes(ref, sem):
    pltpu.make_async_copy(ref, ref, sem).wait()


def kernel(
    sizes,
    lower_hbm, inner_hbm, inverse_hbm, known_hbm, right_hbm,
    out_ref,
    lower_v, known_v, inverse_v, inverse_high, inverse_low, right_v, inner_v,
    p_send, p_recv, acc_v, red_v, count_v, u_send, u_recv, s_v,
    in_sem, known_sem,
    p_ssem, p_rsem, l_ssem, l_rsem, u_ssem, u_rsem, g_ssem, g_rsem,
    a_ssem, a_rsem, b_ssem, b_rsem,
):
    X, Y, Z = sizes
    row = lax.axis_index("row")
    col = lax.axis_index("col")
    x = lax.axis_index("depth")
    y = row // Z
    z = row % Z
    plane = X * Z
    me = x * Z + z
    step_rows = X * Y * Z * T
    quarter = step_rows // X // Y
    n_chunks = known_sem.shape[0]
    width = Z * LANES // n_chunks

    def place(px, py, pz):
        return (py * Z + pz, col, px)

    def z_lanes(pz):
        return pl.ds(pl.multiple_of(pz * LANES, LANES), LANES)

    lower_in = pltpu.make_async_copy(lower_hbm, lower_v, in_sem.at[0])
    lower_in.start()
    known_in = []
    for n in range(n_chunks):
        cut = pl.ds(n * width, width)
        copy = pltpu.make_async_copy(known_hbm.at[:, cut], known_v.at[:, cut], known_sem.at[n])
        copy.start()
        known_in.append(copy)
    right_in = pltpu.make_async_copy(right_hbm, right_v, in_sem.at[1])
    right_in.start()
    inner_in = pltpu.make_async_copy(inner_hbm, inner_v.at[:, z], in_sem.at[2])
    inner_in.start()
    inverse_in = pltpu.make_async_copy(inverse_hbm, inverse_v, in_sem.at[3])
    inverse_in.start()

    barrier = pltpu.get_barrier_semaphore()

    def greet_xz(o, carry):
        there = lax.rem(me + o, plane)
        pl.semaphore_signal(
            barrier, inc=1, device_id=place(there // Z, y, there % Z), device_id_type=MESH
        )
        return carry

    lax.fori_loop(1, plane, greet_xz, 0)

    def greet_xy(o, carry):
        there = lax.rem(y + 1 + o // X, Y)
        pl.semaphore_signal(barrier, inc=1, device_id=place(o % X, there, z), device_id_type=MESH)
        return carry

    lax.fori_loop(0, (Y - 1) * X, greet_xy, 0)

    lower_in.wait()
    right_in.wait()
    rows = 3 * X * T
    lower_high, lower_low = split(lower_v[...].reshape(rows, lower_v.shape[2]))
    lower_both = jnp.concatenate([lower_high, lower_low], axis=0)
    for n in range(n_chunks):
        known_in[n].wait()
        k_high, k_low = split(known_v[:, n * width : (n + 1) * width])
        first = dot(lower_both, k_high)
        prod = first[:rows] + (first[rows:] + dot(lower_high, k_low))
        for k in range(3):
            for xd in range(X):
                base = (k * X + xd) * T
                mine = right_v[k, xd * T : (xd + 1) * T, n * width : (n + 1) * width]
                value = jnp.where(x == xd, mine, 0.0) - prod[base : base + T]
                for zz in range(width // LANES):
                    zd = n * (width // LANES) + zz
                    p_send[k, xd * Z + zd] = value[:, zz * LANES : (zz + 1) * LANES]
    inner_in.wait()
    pl.semaphore_wait(barrier, plane - 1 + (Y - 1) * X)

    def send_p(first, count, slot):
        def body(o, carry):
            there = lax.rem(me + o, plane)
            pltpu.make_async_remote_copy(
                p_send.at[pl.ds(first, count), there],
                p_recv.at[pl.ds(first, count), me],
                p_ssem.at[slot],
                p_rsem.at[slot],
                device_id=place(there // Z, y, there % Z),
                device_id_type=MESH,
            ).start()
            return carry

        lax.fori_loop(1, plane, body, 0)

    def send_inner(which):
        def body(o, carry):
            pltpu.make_async_remote_copy(
                inner_v.at[which, z],
                inner_v.at[which, z],
                l_ssem.at[which],
                l_rsem.at[which],
                device_id=place(x, y, lax.rem(z + o, Z)),
                device_id_type=MESH,
            ).start()
            return carry

        lax.fori_loop(1, Z, body, 0)

    send_p(0, 1, 0)
    send_inner(0)
    send_p(1, 2, 1)
    send_inner(1)
    send_inner(2)
    for k in range(3):
        p_recv[k, me] = p_send[k, me]

    def p_sum(k):
        total = p_recv[k, 0:Z]
        for xs in range(1, X):
            total = total + p_recv[k, xs * Z : (xs + 1) * Z]
        return total

    def gather(k, value):
        acc_v[k] = value
        red_v[k, y, :, x] = value

        def body(o, carry):
            there = lax.rem(y * X + x + o, X * Y)
            pltpu.make_async_remote_copy(
                acc_v.at[k],
                red_v.at[k, y, :, x],
                g_ssem.at[k],
                g_rsem.at[k],
                device_id=place(there % X, there // X, z),
                device_id_type=MESH,
            ).start()
            return carry

        lax.fori_loop(1, X * Y, body, 0)

    def solve(k):
        wait_bytes(count_v.at[pl.ds(0, X * Y - 1)], g_rsem.at[k])
        value = three_pass(
            inverse_high[k], inverse_low[k], red_v[k].reshape(step_rows, LANES)
        )
        s_v[k] = value
        out_ref[k, :, z_lanes(z)] = value

    def apply_inner(which, k):
        high, low = split(inner_v[which].reshape(Z * X * T, inner_v.shape[3]))
        return three_pass(high, low, s_v[k]).reshape(Z, X, T, LANES)

    def send_update(j, value):
        for xd in range(X):
            u_send[j, xd] = value[:, xd]
        u_recv[j, x] = u_send[j, x]

        def body(o, carry):
            there = lax.rem(x + o, X)
            pltpu.make_async_remote_copy(
                u_send.at[j, there],
                u_recv.at[j, x],
                u_ssem.at[j],
                u_rsem.at[j],
                device_id=place(there, y, z),
                device_id_type=MESH,
            ).start()
            return carry

        lax.fori_loop(1, X, body, 0)

    def update_sum(j):
        wait_bytes(u_recv.at[j, pl.ds(0, X - 1)], u_rsem.at[j])
        total = u_recv[j, 0]
        for xs in range(1, X):
            total = total + u_recv[j, xs]
        return total

    own_rows = pl.ds(pl.multiple_of(y * quarter, T), quarter)

    def spread_z(k):
        def body(o, carry):
            pltpu.make_async_remote_copy(
                s_v.at[k, own_rows],
                out_ref.at[k, own_rows, z_lanes(z)],
                a_ssem.at[k],
                a_rsem.at[k, o],
                device_id=place(x, y, lax.rem(z + o, Z)),
                device_id_type=MESH,
            ).start()
            return carry

        lax.fori_loop(1, Z, body, 0)

    def spread_y(k):
        def body(o, carry):
            block = out_ref.at[k, own_rows, z_lanes(lax.rem(z + Z - o, Z))]
            wait_bytes(block, a_rsem.at[k, o])
            for p in range(1, Y):
                pltpu.make_async_remote_copy(
                    block,
                    block,
                    b_ssem.at[k],
                    b_rsem.at[k],
                    device_id=place(x, lax.rem(y + p, Y), z),
                    device_id_type=MESH,
                ).start()
            return carry

        lax.fori_loop(1, Z, body, 0)

    wait_bytes(p_recv.at[pl.ds(0, 1), pl.ds(0, plane - 1)], p_rsem.at[0])
    gather(0, p_sum(0))
    inverse_in.wait()
    for k in range(3):
        high, low = split(inverse_v[k])
        inverse_high[k] = high
        inverse_low[k] = low
    solve(0)

    wait_bytes(inner_v.at[0, pl.ds(0, Z - 1)], l_rsem.at[0])
    send_update(0, apply_inner(0, 0))
    spread_z(0)
    wait_bytes(p_recv.at[pl.ds(1, 2), pl.ds(0, plane - 1)], p_rsem.at[1])
    wait_bytes(inner_v.at[1, pl.ds(0, Z - 1)], l_rsem.at[1])
    early = apply_inner(1, 0)
    gather(1, p_sum(1) - update_sum(0))
    spread_y(0)
    wait_bytes(inner_v.at[2, pl.ds(0, Z - 1)], l_rsem.at[2])
    solve(1)

    send_update(1, early + apply_inner(2, 1))
    spread_z(1)
    gather(2, p_sum(2) - update_sum(1))
    spread_y(1)
    solve(2)
    spread_z(2)
    spread_y(2)

    wait_bytes(p_send.at[pl.ds(0, 1), pl.ds(0, plane - 1)], p_ssem.at[0])
    wait_bytes(p_send.at[pl.ds(1, 2), pl.ds(0, plane - 1)], p_ssem.at[1])
    for k in range(3):
        wait_bytes(inner_v.at[k, pl.ds(0, Z - 1)], l_ssem.at[k])
        wait_bytes(count_v.at[pl.ds(0, X * Y - 1)], g_ssem.at[k])
        wait_bytes(out_ref.at[k, pl.ds(0, quarter), pl.ds(0, (Z - 1) * LANES)], a_ssem.at[k])
        forwarded = out_ref.at[k, pl.ds(0, (Y - 1) * quarter), pl.ds(0, (Z - 1) * LANES)]
        wait_bytes(forwarded, b_ssem.at[k])
        wait_bytes(forwarded, b_rsem.at[k])
    for j in range(2):
        wait_bytes(u_send.at[j, pl.ds(0, X - 1)], u_ssem.at[j])


def on_device(sizes, lower_prev, inner_blocks, diag_inverse, known_rows, right_sides):
    X, Y, Z = sizes
    step_rows = X * Y * Z * T
    f32 = jnp.float32
    dma = pltpu.SemaphoreType.DMA
    return pl.pallas_call(
        functools.partial(kernel, sizes),
        out_shape=jax.ShapeDtypeStruct((3, step_rows // X, Z * LANES), f32),
        in_specs=[pl.BlockSpec(memory_space=pl.ANY)] * 5,
        out_specs=pl.BlockSpec(memory_space=pltpu.VMEM),
        scratch_shapes=[
            pltpu.VMEM(lower_prev.shape, f32),
            pltpu.VMEM(known_rows.shape, f32),
            pltpu.VMEM(diag_inverse.shape, f32),
            pltpu.VMEM(diag_inverse.shape, jnp.bfloat16),
            pltpu.VMEM(diag_inverse.shape, jnp.bfloat16),
            pltpu.VMEM(right_sides.shape, f32),
            pltpu.VMEM((3, Z) + inner_blocks.shape[1:], f32),
            pltpu.VMEM((3, X * Z, T, LANES), f32),
            pltpu.VMEM((3, X * Z, T, LANES), f32),
            pltpu.VMEM((3, Z, T, LANES), f32),
            pltpu.VMEM((3, Y, Z, X, T, LANES), f32),
            pltpu.VMEM((X * Y, Z, T, LANES), f32),
            pltpu.VMEM((2, X, Z, T, LANES), f32),
            pltpu.VMEM((2, X, Z, T, LANES), f32),
            pltpu.VMEM((3, step_rows // X, LANES), f32),
            dma((4,)),
            dma((max(1, Z // 2),)),
            dma((2,)), dma((2,)),
            dma((3,)), dma((3,)),
            dma((2,)), dma((2,)),
            dma((3,)), dma((3,)),
            dma((3,)), dma((3, Z)),
            dma((3,)), dma((3,)),
        ],
        compiler_params=pltpu.CompilerParams(
            collective_id=0, has_side_effects=True, vmem_limit_bytes=56 * 1024 * 1024
        ),
    )(lower_prev, inner_blocks, diag_inverse, known_rows, right_sides)


def solution(mesh):
    X = mesh.shape["depth"]
    Y = 4 if mesh.shape["row"] == 32 else 2
    sizes = (X, Y, mesh.shape["row"] // Y)
    placed = (
        P(None, "row", "depth"),
        P(None, "row", "depth"),
        P(None, "depth", None),
        P("depth", "col"),
        P(None, "row", "col"),
    )
    return jax.shard_map(
        functools.partial(on_device, sizes),
        mesh=mesh,
        in_specs=placed,
        out_specs=P(None, "depth", "col"),
        check_vma=False,
    )
```

time: 627 us -> 83.7 us (0.13)
  waiting for transfers between devices: 584 us -> 0 us
  Pallas kernels: 0 us -> 79.6 us
  matrix products: 20.5 us -> 0 us
  between operations: 13.5 us -> 0.01 us
    psum x6 -> x0, waiting for transfers between devices: 584 us -> none  [the longest x3 454 us: on_device(): solution = lax.psum(partial_sum, 'row')]
    pallas_call x0 -> x1, Pallas kernels: none -> 79.6 us  [on_device(): pl.pallas_call(functools.partial(kernel, sizes), out_shape=jax.ShapeDtype...]
    dot_general x7 -> x0, matrix products: 20.5 us -> none  [the longest x3 8.93 us: on_device(): jnp.dot(columns, reduced, precision=highest, preferred_element_type=jnp.f...]
  transfers between devices with their start and end apart: 6 -> 0, of which waited for: 6 -> 0; matrix products, arithmetic and copies ran while one was open for 1% -> 0% of each run, Pallas kernels for 0% -> 0%
where the time goes in v1:
time: 83.7 us; the launch traced here: 83.6 us
  Pallas kernels  79.6 us (95%)
  local copies, waits for them, and re-layouts  3.97 us (5%)
    pallas_call x1, Pallas kernels, on_device(): pl.pallas_call(functools.partial(kernel, sizes), out_shape=jax.ShapeDtype...  79.6 us
    unnamed x1, local copies, waits for them, and re-layouts  3.97 us

profile of v1, /device:TPU:2, one launch (start us, length us, event | category | flops | bytes accessed | tf_op | source)
XLA Modules:
  0.0 83.6 jit_solution(4679200694583050665)
XLA Ops:
  0.0 79.6 %shard_map.55 = f32[3,256,1024]{2,1,0:T(8,128)} custom-call(f32[3,32,1024]{2,1,0:T(8,128)} %lower_hbm.1, f32[3,32,256]{2,1,0:T(8,128)} %inner_hbm.1, f32[3,256,1024]{2,1,0:T(8,128)} %inverse_hbm.1, f32[1024,1024]{1,0:T(8,128)} %known_hbm.1, f32[3,32,1024]{2,1,0:T(8,128)} %right_hbm.1), custom_call_target="tpu_custom_call" | custom-call | tf_op jit(solution)/shard_map/pallas_call | solution.py:297
  79.6 4.0 %copy.7 = f32[3,256,1024]{2,1,0:T(8,128)} copy(f32[3,256,1024]{2,1,0:T(8,128)} %shard_map.55) | data formatting | bytes 6291456

commit v2 on v0

v2 whole, which is shorter than its diff:
```python
import functools

import jax
import jax.numpy as jnp
from jax import lax
from jax.experimental import pallas as pl
from jax.experimental.pallas import tpu as pltpu
from jax.sharding import PartitionSpec as P

MESH = pl.DeviceIdType.MESH
T = 8
LANES = 128


def split(value):
    high = value.astype(jnp.bfloat16)
    low = (value - high.astype(jnp.float32)).astype(jnp.bfloat16)
    return high, low


def dot(a, b):
    return jnp.dot(a, b, preferred_element_type=jnp.float32)


def three_pass(a_high, a_low, b):
    b_high, b_low = split(b)
    width = b.shape[1]
    both = dot(a_high, jnp.concatenate([b_high, b_low], axis=1))
    return both[:, :width] + (both[:, width:] + dot(a_low, b_high))


def wait_bytes(ref, sem):
    pltpu.make_async_copy(ref, ref, sem).wait()


def kernel(
    sizes,
    lower_hbm, inner_hbm, inverse_hbm, known_hbm, right_hbm,
    out_ref,
    lower_v, known_v, inverse_v, inverse_high, inverse_low, right_v, inner_v,
    p_send, p_recv, q_send, q_recv, acc_v, red_v, u_send, u_recv,
    in_sem, known_sem,
    p_ssem, p_rsem, q_ssem, q_rsem, l_ssem, l_rsem, u_ssem, u_rsem, g_ssem, g_rsem,
    r_ssem, r_rsem, a_ssem, a_rsem, b_ssem, b_rsem,
):
    X, Y, Z = sizes
    row = lax.axis_index("row")
    col = lax.axis_index("col")
    x = lax.axis_index("depth")
    y = row // Z
    z = row % Z
    step_rows = X * Y * Z * T
    own = step_rows // X
    quarter = own // Y
    n_chunks = known_sem.shape[0]
    width = Z * LANES // n_chunks

    def on_x(o):
        return (row, col, lax.rem(x + o, X))

    def on_y(o):
        return (lax.rem(y + o, Y) * Z + z, col, x)

    def on_z(o):
        return (y * Z + lax.rem(z + o, Z), col, x)

    def z_lanes(pz):
        return pl.ds(pl.multiple_of(pz * LANES, LANES), LANES)

    def send(src, dst, ssem, rsem, device):
        pltpu.make_async_remote_copy(
            src, dst, ssem, rsem, device_id=device, device_id_type=MESH
        ).start()

    lower_in = pltpu.make_async_copy(lower_hbm, lower_v, in_sem.at[0])
    lower_in.start()
    known_in = []
    for n in range(n_chunks):
        cut = pl.ds(n * width, width)
        copy = pltpu.make_async_copy(known_hbm.at[:, cut], known_v.at[:, cut], known_sem.at[n])
        copy.start()
        known_in.append(copy)
    right_in = pltpu.make_async_copy(right_hbm, right_v, in_sem.at[1])
    right_in.start()
    inner_in = pltpu.make_async_copy(inner_hbm, inner_v.at[:, z], in_sem.at[2])
    inner_in.start()
    inverse_in = pltpu.make_async_copy(inverse_hbm, inverse_v, in_sem.at[3])
    inverse_in.start()

    red_v[...] = jnp.zeros_like(red_v)

    barrier = pltpu.get_barrier_semaphore()
    for on, extent in ((on_x, X), (on_z, Z), (on_y, Y)):
        for o in range(1, extent):
            pl.semaphore_signal(barrier, inc=1, device_id=on(o), device_id_type=MESH)

    lower_in.wait()
    right_in.wait()
    rows = 3 * X * T
    lower_high, lower_low = split(lower_v[...].reshape(rows, lower_v.shape[2]))
    lower_both = jnp.concatenate([lower_high, lower_low], axis=0)
    for n in range(n_chunks):
        known_in[n].wait()
        cut = slice(n * width, (n + 1) * width)
        k_high, k_low = split(known_v[:, cut])
        first = dot(lower_both, k_high)
        prod = first[:rows] + (first[rows:] + dot(lower_high, k_low))
        for k in range(3):
            for xd in range(X):
                base = (k * X + xd) * T
                mine = right_v[k, xd * T : (xd + 1) * T, cut]
                p_send[k, xd, :, cut] = jnp.where(x == xd, mine, 0.0) - prod[base : base + T]
    pl.semaphore_wait(barrier, X - 1 + Y - 1 + Z - 1)

    steps = (pl.ds(0, 1), pl.ds(1, 2))

    def p_to_x(slot):
        for o in range(1, X):
            there = lax.rem(x + o, X)
            send(
                p_send.at[steps[slot], there], p_recv.at[steps[slot], o],
                p_ssem.at[slot], p_rsem.at[slot], on_x(o),
            )

    def p_to_z(slot):
        wait_bytes(p_recv.at[steps[slot], pl.ds(1, X - 1)], p_rsem.at[slot])
        for k in ((0,), (1, 2))[slot]:
            total = p_send[k, x]
            for o in range(1, X):
                total = total + p_recv[k, o]
            for zd in range(Z):
                q_send[k, zd] = total[:, zd * LANES : (zd + 1) * LANES]
            q_recv[k, z] = q_send[k, z]
        for o in range(1, Z):
            there = lax.rem(z + o, Z)
            send(
                q_send.at[steps[slot], there], q_recv.at[steps[slot], z],
                q_ssem.at[slot], q_rsem.at[slot], on_z(o),
            )

    def q_wait(slot):
        wait_bytes(q_recv.at[steps[slot], pl.ds(0, Z - 1)], q_rsem.at[slot])

    def inner_to_z(slot):
        for o in range(1, Z):
            block = inner_v.at[steps[slot], z]
            send(block, block, l_ssem.at[slot], l_rsem.at[slot], on_z(o))

    def inner_wait(slot):
        wait_bytes(inner_v.at[steps[slot], pl.ds(0, Z - 1)], l_rsem.at[slot])

    def split_inverse(k):
        high, low = split(inverse_v[k])
        inverse_high[k] = high
        inverse_low[k] = low

    places = X * Y
    here = y * X + x

    def gather(k, value):
        acc_v[k] = value
        red_v[k, y, :, x] = value

        def body(o, carry):
            there = lax.rem(here + o, places)

            @pl.when(there % X >= y)
            def _():
                send(
                    acc_v.at[k], red_v.at[k, y, :, x],
                    g_ssem.at[k, o], g_rsem.at[k, here],
                    ((there // X) * Z + z, col, there % X),
                )

            return carry

        lax.fori_loop(1, places, body, 0)

    def gather_wait(k):
        def body(source, carry):
            @pl.when((source // X <= x) & (source != here))
            def _():
                wait_bytes(red_v.at[k, source // X, :, source % X], g_rsem.at[k, source])

            return carry

        lax.fori_loop(0, places, body, 0)

    def gather_done(k):
        def body(o, carry):
            @pl.when(lax.rem(here + o, places) % X >= y)
            def _():
                wait_bytes(acc_v.at[k], g_ssem.at[k, o])

            return carry

        lax.fori_loop(1, places, body, 0)

    def solve(k):
        gather_wait(k)
        value = three_pass(
            inverse_high[k], inverse_low[k], red_v[k].reshape(step_rows, LANES)
        )
        out_ref[k, :, z_lanes(z)] = value
        return value

    def apply_inner(which, value):
        high, low = split(inner_v[which].reshape(Z * X * T, inner_v.shape[3]))
        return three_pass(high, low, value).reshape(Z, X, T, LANES)

    def update_to_x(j, value):
        for xd in range(X):
            u_send[j, xd] = value[:, xd]
        for o in range(1, X):
            there = lax.rem(x + o, X)
            send(u_send.at[j, there], u_recv.at[j, o], u_ssem.at[j], u_rsem.at[j], on_x(o))

    def update_sum(j):
        wait_bytes(u_recv.at[j, pl.ds(1, X - 1)], u_rsem.at[j])
        total = u_send[j, x]
        for o in range(1, X):
            total = total + u_recv[j, o]
        return total

    hops = Z // 2
    half = own // 2

    def ring_block(k, hop, way):
        lanes = z_lanes(lax.rem(z + (Z - hop if way == 0 else hop), Z))
        if hop == hops - 1:
            return out_ref.at[k, pl.ds(way * half, half), lanes]
        return out_ref.at[k, :, lanes]

    def ring_wait(k, hop):
        for way in range(2):
            came = ring_block(k, hop, way)
            wait_bytes(came, r_rsem.at[k, hop, way])

    def ring(k, hop):
        if hop >= hops:
            return
        if hop > 0:
            ring_wait(k, hop - 1)
        for way in range(2):
            block = ring_block(k, hop, way)
            send(
                block, block, r_ssem.at[k, hop, way], r_rsem.at[k, hop, way],
                on_z(1 if way == 0 else Z - 1),
            )

    def ring_done(k):
        ring_wait(k, hops - 1)
        for hop in range(hops):
            for way in range(2):
                wait_bytes(ring_block(k, hop, way), r_ssem.at[k, hop, way])

    last = 2
    own_rows = pl.ds(pl.multiple_of(y * quarter, T), quarter)
    near = sorted(range(1, Z), key=lambda o: (min(o, Z - o), o))

    def spread_z():
        block = out_ref.at[last, own_rows, z_lanes(z)]
        for o in near:
            send(block, block, a_ssem.at[0], a_rsem.at[o], on_z(o))

    def spread_y(offsets):
        for o in offsets:
            block = out_ref.at[last, own_rows, z_lanes(lax.rem(z + Z - o, Z))]
            wait_bytes(block, a_rsem.at[o])
            for p in range(1, Y):
                send(block, block, b_ssem.at[0], b_rsem.at[0], on_y(p))

    p_to_x(0)
    p_to_x(1)
    inner_in.wait()
    p_to_z(0)
    inner_to_z(0)
    p_to_z(1)
    inverse_in.wait()
    split_inverse(0)
    q_wait(0)
    gather(0, q_recv[0])
    inner_to_z(1)
    split_inverse(1)
    split_inverse(2)
    solved = solve(0)

    inner_wait(0)
    update_to_x(0, apply_inner(0, solved))
    ring(0, 0)
    q_wait(1)
    inner_wait(1)
    early = apply_inner(1, solved)
    gather(1, q_recv[1] - update_sum(0))
    ring(0, 1)
    solved = solve(1)

    update_to_x(1, early + apply_inner(2, solved))
    ring(1, 0)
    ring(0, 2)
    gather(2, q_recv[2] - update_sum(1))
    ring(1, 1)
    ring(0, 3)
    solve(2)
    spread_z()
    ring(1, 2)
    spread_y(near[:4])
    ring(1, 3)
    spread_y(near[4:])

    ring_done(0)
    ring_done(1)
    for slot in range(2):
        wait_bytes(p_send.at[steps[slot], pl.ds(0, X - 1)], p_ssem.at[slot])
        wait_bytes(q_send.at[steps[slot], pl.ds(0, Z - 1)], q_ssem.at[slot])
        wait_bytes(inner_v.at[steps[slot], pl.ds(0, Z - 1)], l_ssem.at[slot])
        wait_bytes(u_send.at[slot, pl.ds(0, X - 1)], u_ssem.at[slot])
    for k in range(3):
        gather_done(k)
    lanes = pl.ds(0, (Z - 1) * LANES)
    wait_bytes(out_ref.at[last, pl.ds(0, quarter), lanes], a_ssem.at[0])
    passed_on = out_ref.at[last, pl.ds(0, (Y - 1) * quarter), lanes]
    wait_bytes(passed_on, b_ssem.at[0])
    wait_bytes(passed_on, b_rsem.at[0])


def on_device(sizes, lower_prev, inner_blocks, diag_inverse, known_rows, right_sides):
    X, Y, Z = sizes
    step_rows = X * Y * Z * T
    f32 = jnp.float32
    dma = pltpu.SemaphoreType.DMA
    return pl.pallas_call(
        functools.partial(kernel, sizes),
        out_shape=pltpu.VMEM((3, step_rows // X, Z * LANES), f32),
        in_specs=[pl.BlockSpec(memory_space=pl.ANY)] * 5,
        out_specs=pl.BlockSpec(memory_space=pltpu.VMEM),
        scratch_shapes=[
            pltpu.VMEM(lower_prev.shape, f32),
            pltpu.VMEM(known_rows.shape, f32),
            pltpu.VMEM(diag_inverse.shape, f32),
            pltpu.VMEM(diag_inverse.shape, jnp.bfloat16),
            pltpu.VMEM(diag_inverse.shape, jnp.bfloat16),
            pltpu.VMEM(right_sides.shape, f32),
            pltpu.VMEM((3, Z) + inner_blocks.shape[1:], f32),
            pltpu.VMEM((3, X, T, Z * LANES), f32),
            pltpu.VMEM((3, X, T, Z * LANES), f32),
            pltpu.VMEM((3, Z, T, LANES), f32),
            pltpu.VMEM((3, Z, T, LANES), f32),
            pltpu.VMEM((3, Z, T, LANES), f32),
            pltpu.VMEM((3, Y, Z, X, T, LANES), f32),
            pltpu.VMEM((2, X, Z, T, LANES), f32),
            pltpu.VMEM((2, X, Z, T, LANES), f32),
            dma((4,)),
            dma((max(1, Z // 2),)),
            dma((2,)), dma((2,)),
            dma((2,)), dma((2,)),
            dma((2,)), dma((2,)),
            dma((2,)), dma((2,)),
            dma((3, X * Y)), dma((3, X * Y)),
            dma((2, Z // 2, 2)), dma((2, Z // 2, 2)),
            dma((1,)), dma((Z,)),
            dma((1,)), dma((1,)),
        ],
        compiler_params=pltpu.CompilerParams(
            collective_id=0, has_side_effects=True, vmem_limit_bytes=56 * 1024 * 1024
        ),
    )(lower_prev, inner_blocks, diag_inverse, known_rows, right_sides)


def solution(mesh):
    X = mesh.shape["depth"]
    Y = 4 if mesh.shape["row"] == 32 else 2
    sizes = (X, Y, mesh.shape["row"] // Y)
    placed = (
        P(None, "row", "depth"),
        P(None, "row", "depth"),
        P(None, "depth", None),
        P("depth", "col"),
        P(None, "row", "col"),
    )
    return jax.shard_map(
        functools.partial(on_device, sizes),
        mesh=mesh,
        in_specs=placed,
        out_specs=P(None, "depth", "col"),
        check_vma=False,
    )
```

time: 627 us -> 71.3 us (0.11)
  waiting for transfers between devices: 584 us -> 0 us
  Pallas kernels: 0 us -> 69.2 us
  matrix products: 20.5 us -> 0 us
  between operations: 13.5 us -> 0.01 us
    psum x6 -> x0, waiting for transfers between devices: 584 us -> none  [the longest x3 454 us: on_device(): solution = lax.psum(partial_sum, 'row')]
    pallas_call x0 -> x1, Pallas kernels: none -> 69.2 us  [on_device(): pl.pallas_call(functools.partial(kernel, sizes), out_shape=pltpu.VMEM((3,...]
    dot_general x7 -> x0, matrix products: 20.5 us -> none  [the longest x3 8.93 us: on_device(): jnp.dot(columns, reduced, precision=highest, preferred_element_type=jnp.f...]
  transfers between devices with their start and end apart: 6 -> 0, of which waited for: 6 -> 0; matrix products, arithmetic and copies ran while one was open for 1% -> 0% of each run, Pallas kernels for 0% -> 0%
where the time goes in v2:
time: 71.3 us; the launch traced here: 70.8 us
  Pallas kernels  69.2 us (97%)
  local copies, waits for them, and re-layouts  1.67 us (2%)
    pallas_call x1, Pallas kernels, on_device(): pl.pallas_call(functools.partial(kernel, sizes), out_shape=pltpu.VMEM((3,...  69.2 us
    unnamed x1, local copies, waits for them, and re-layouts  1.67 us

profile of v2, /device:TPU:2, one launch (start us, length us, event | category | flops | bytes accessed | tf_op | source)
XLA Modules:
  0.0 70.8 jit_solution(13626479858346327271)
XLA Ops:
  0.0 69.2 %shard_map.55 = f32[3,256,1024]{2,1,0:T(8,128)S(1)} custom-call(f32[3,32,1024]{2,1,0:T(8,128)} %lower_hbm.1, f32[3,32,256]{2,1,0:T(8,128)} %inner_hbm.1, f32[3,256,1024]{2,1,0:T(8,128)} %inverse_hbm.1, f32[1024,1024]{1,0:T(8,128)} %known_hbm.1, f32[3,32,1024]{2,1,0:T(8,128)} %right_hbm.1), custom_call_target="tpu_custom_call" | custom-call | tf_op jit(solution)/shard_map/pallas_call | solution.py:332
  69.2 1.7 %copy.7 = f32[3,256,1024]{2,1,0:T(8,128)} copy(f32[3,256,1024]{2,1,0:T(8,128)S(1)} %shard_map.55) | data formatting | bytes 6291456

commit v3 on v2

v3 whole, which is shorter than its diff:
```python
import functools

import jax
import jax.numpy as jnp
from jax import lax
from jax.experimental import pallas as pl
from jax.experimental.pallas import tpu as pltpu
from jax.sharding import PartitionSpec as P

MESH = pl.DeviceIdType.MESH
T = 8
LANES = 128


def split(value):
    high = value.astype(jnp.bfloat16)
    low = (value - high.astype(jnp.float32)).astype(jnp.bfloat16)
    return high, low


def dot(a, b):
    return jnp.dot(a, b, preferred_element_type=jnp.float32)


def three_pass(a_high, a_low, b):
    b_high, b_low = split(b)
    width = b.shape[1]
    both = dot(a_high, jnp.concatenate([b_high, b_low], axis=1))
    return both[:, :width] + (both[:, width:] + dot(a_low, b_high))


def wait_bytes(ref, sem):
    pltpu.make_async_copy(ref, ref, sem).wait()


def kernel(
    sizes,
    lower_hbm, inner_hbm, inverse_hbm, known_hbm, right_hbm,
    out_ref,
    lower_v, known_v, inverse_v, inverse_high, inverse_low, right_v, inner_v,
    first_send, first_recv, p_send, p_recv, q_send, q_recv, acc_v, red_v, u_send, u_recv,
    in_sem, known_sem,
    first_ssem, first_rsem, p_ssem, p_rsem, q_ssem, q_rsem, l_ssem, l_rsem, h_ssem, h_rsem, u_ssem, u_rsem, g_ssem, g_rsem,
    a_ssem, a_rsem, b_ssem, b_rsem,
):
    X, Y, Z = sizes
    reach = (1, 1, 2)
    row = lax.axis_index("row")
    col = lax.axis_index("col")
    x = lax.axis_index("depth")
    y = row // Z
    z = row % Z
    step_rows = X * Y * Z * T
    own = step_rows // X
    quarter = own // Y
    n_chunks = known_sem.shape[0]
    width = Z * LANES // n_chunks

    def on_x(o):
        return (row, col, lax.rem(x + o, X))

    def on_y(o):
        return (lax.rem(y + o, Y) * Z + z, col, x)

    def on_z(o):
        return (y * Z + lax.rem(z + o, Z), col, x)

    def z_lanes(pz):
        return pl.ds(pl.multiple_of(pz * LANES, LANES), LANES)

    def send(src, dst, ssem, rsem, device):
        pltpu.make_async_remote_copy(
            src, dst, ssem, rsem, device_id=device, device_id_type=MESH
        ).start()

    def far(o, extent):
        return min(o, extent - o)

    def far_first(extent):
        return sorted(range(1, extent), key=lambda o: -far(o, extent))

    xz = sorted(
        ((dx, dz) for dx in range(X) for dz in range(Z) if dx or dz),
        key=lambda d: -(far(d[0], X) + far(d[1], Z)),
    )
    xy = sorted(
        ((dx, dy) for dx in range(X) for dy in range(Y) if dx or dy),
        key=lambda d: -(far(d[0], X) + far(d[1], Y)),
    )

    barrier = pltpu.get_barrier_semaphore()
    for dx, dz in xz:
        device = (y * Z + lax.rem(z + dz, Z), col, lax.rem(x + dx, X))
        pl.semaphore_signal(barrier, inc=1, device_id=device, device_id_type=MESH)
    for o in range(1, Y):
        pl.semaphore_signal(barrier, inc=1, device_id=on_y(o), device_id_type=MESH)

    other_core = (row, 1 - col, x)
    pl.semaphore_signal(barrier, inc=1, device_id=other_core, device_id_type=MESH)

    lower_in = pltpu.make_async_copy(lower_hbm, lower_v, in_sem.at[0])
    lower_in.start()
    known_in = []
    for n in range(n_chunks):
        cut = pl.ds(n * width, width)
        copy = pltpu.make_async_copy(known_hbm.at[:, cut], known_v.at[:, cut], known_sem.at[n])
        copy.start()
        known_in.append(copy)
    right_in = pltpu.make_async_copy(right_hbm, right_v, in_sem.at[1])
    right_in.start()
    inner_in = pltpu.make_async_copy(inner_hbm, inner_v.at[:, 0], in_sem.at[2])
    inner_in.start()
    inverse_in = pltpu.make_async_copy(inverse_hbm, inverse_v, in_sem.at[3])
    inverse_in.start()

    for yy in range(1, Y):
        @pl.when(yy > x)
        def _():
            red_v[:, yy] = jnp.zeros_like(red_v[:, yy])

    lower_in.wait()
    right_in.wait()
    rows = 3 * X * T
    lower_high, lower_low = split(lower_v[...].reshape(rows, lower_v.shape[2]))
    lower_both = jnp.concatenate([lower_high, lower_low], axis=0)
    for n in range(n_chunks):
        known_in[n].wait()
        cut = slice(n * width, (n + 1) * width)
        k_high, k_low = split(known_v[:, cut])
        first = dot(lower_both, k_high)
        prod = first[:rows] + (first[rows:] + dot(lower_high, k_low))
        for k in range(3):
            for xd in range(X):
                base = (k * X + xd) * T
                mine = right_v[k, xd * T : (xd + 1) * T, cut]
                value = jnp.where(x == xd, mine, 0.0) - prod[base : base + T]
                if k > 0:
                    p_send[k - 1, xd, :, cut] = value
                else:
                    for zz in range(width // LANES):
                        zd = n * (width // LANES) + zz
                        first_send[xd * Z + zd] = value[:, zz * LANES : (zz + 1) * LANES]
    inverse_in.wait()
    for k in range(3):
        high, low = split(inverse_v[k])
        inverse_high[k] = high
        inverse_low[k] = low
    inner_in.wait()
    pl.semaphore_wait(barrier, len(xz) + Y)

    steps = (pl.ds(0, 1), pl.ds(1, 2))
    me = x * Z + z

    def first_to_xz():
        for dx, dz in xz:
            xd = lax.rem(x + dx, X)
            zd = lax.rem(z + dz, Z)
            send(
                first_send.at[xd * Z + zd], first_recv.at[me],
                first_ssem.at[0], first_rsem.at[0], (y * Z + zd, col, xd),
            )
        first_recv[me] = first_send[me]

    def first_sum():
        wait_bytes(first_recv.at[pl.ds(0, X * Z - 1)], first_rsem.at[0])
        total = first_recv[0:Z]
        for xs in range(1, X):
            total = total + first_recv[xs * Z : (xs + 1) * Z]
        return total

    def p_to_x():
        for o in far_first(X):
            there = lax.rem(x + o, X)
            send(p_send.at[:, there], p_recv.at[:, o], p_ssem.at[0], p_rsem.at[0], on_x(o))

    def p_to_z():
        wait_bytes(p_recv.at[:, pl.ds(1, X - 1)], p_rsem.at[0])
        for k in range(2):
            total = p_send[k, x]
            for o in range(1, X):
                total = total + p_recv[k, o]
            for zd in range(Z):
                q_send[k, zd] = total[:, zd * LANES : (zd + 1) * LANES]
            q_recv[k, z] = q_send[k, z]
        for o in far_first(Z):
            there = lax.rem(z + o, Z)
            send(q_send.at[:, there], q_recv.at[:, z], q_ssem.at[0], q_rsem.at[0], on_z(o))

    def q_wait():
        wait_bytes(q_recv.at[:, pl.ds(0, Z - 1)], q_rsem.at[0])

    half = X * T // 2
    my_half = pl.ds(pl.multiple_of(col * half, T), half)

    def inner_to_z(slot):
        for o in far_first(Z):
            send(
                inner_v.at[steps[slot], 0, my_half], inner_v.at[steps[slot], o, my_half],
                l_ssem.at[slot], l_rsem.at[slot], on_z(o),
            )

    def inner_to_core(slot):
        block = inner_v.at[steps[slot], pl.ds(1, Z - 1), my_half]
        wait_bytes(block, l_rsem.at[slot])
        send(block, block, h_ssem.at[slot], h_rsem.at[slot], other_core)

    def inner_wait(slot):
        wait_bytes(inner_v.at[steps[slot], pl.ds(1, Z - 1), my_half], h_rsem.at[slot])

    def gather(k, value):
        acc_v[k] = value
        red_v[k, y, :, x] = value
        for i, (dx, dy) in enumerate(xy):
            xd = lax.rem(x + dx, X)

            @pl.when(xd >= y)
            def _():
                send(
                    acc_v.at[k], red_v.at[k, y, :, x], g_ssem.at[k, i], g_rsem.at[k, i],
                    (lax.rem(y + dy, Y) * Z + z, col, xd),
                )

    def gather_wait(k):
        for i, (dx, dy) in enumerate(xy):
            ys = lax.rem(y + Y - dy, Y)

            @pl.when(ys <= x)
            def _():
                wait_bytes(red_v.at[k, ys, :, lax.rem(x + X - dx, X)], g_rsem.at[k, i])

    def gather_done(k):
        for i, (dx, dy) in enumerate(xy):

            @pl.when(lax.rem(x + dx, X) >= y)
            def _():
                wait_bytes(acc_v.at[k], g_ssem.at[k, i])

    def solve(k):
        gather_wait(k)
        value = three_pass(
            inverse_high[k], inverse_low[k], red_v[k].reshape(step_rows, LANES)
        )
        out_ref[k, :, z_lanes(z)] = value
        return value

    def apply_inner(which, value):
        high, low = split(inner_v[which].reshape(Z * X * T, inner_v.shape[3]))
        return three_pass(high, low, value).reshape(Z, X, T, LANES)

    def update_to_x(j, value):
        for o in range(Z):
            u_send[j, :, lax.rem(z + Z - o, Z)] = value[o]
        for o in far_first(X):
            there = lax.rem(x + o, X)
            send(u_send.at[j, there], u_recv.at[j, o], u_ssem.at[j], u_rsem.at[j], on_x(o))

    def update_sum(j):
        wait_bytes(u_recv.at[j, pl.ds(1, X - 1)], u_rsem.at[j])
        total = u_send[j, x]
        for o in range(1, X):
            total = total + u_recv[j, o]
        return total

    own_rows = pl.ds(pl.multiple_of(y * quarter, T), quarter)

    def spread_z(k, reach):
        block = out_ref.at[k, own_rows, z_lanes(z)]
        for o in far_first(Z):
            if far(o, Z) > reach:
                send(block, block, a_ssem.at[k, o], a_rsem.at[k, o], on_z(o))
        block = out_ref.at[k, :, z_lanes(z)]
        for o in far_first(Z)[::-1]:
            if far(o, Z) <= reach:
                send(block, block, a_ssem.at[k, o], a_rsem.at[k, o], on_z(o))

    def spread_y(k, reach):
        for o in far_first(Z)[::-1]:
            if far(o, Z) > reach:
                block = out_ref.at[k, own_rows, z_lanes(lax.rem(z + Z - o, Z))]
                wait_bytes(block, a_rsem.at[k, o])
                for p in far_first(Y):
                    send(block, block, b_ssem.at[k], b_rsem.at[k], on_y(p))

    def spread_done(k, reach):
        others = 0
        for o in range(1, Z):
            if far(o, Z) > reach:
                wait_bytes(out_ref.at[k, own_rows, z_lanes(z)], a_ssem.at[k, o])
                others += 1
            else:
                block = out_ref.at[k, :, z_lanes(z)]
                wait_bytes(block, a_ssem.at[k, o])
                wait_bytes(block, a_rsem.at[k, o])
        passed_on = out_ref.at[k, pl.ds(0, (Y - 1) * quarter), pl.ds(0, others * LANES)]
        wait_bytes(passed_on, b_ssem.at[k])
        wait_bytes(passed_on, b_rsem.at[k])

    first_to_xz()
    p_to_x()
    inner_to_z(0)
    gather(0, first_sum())
    p_to_z()
    inner_to_z(1)
    inner_to_core(0)
    solved = solve(0)

    inner_wait(0)
    update_to_x(0, apply_inner(0, solved))
    spread_z(0, reach[0])
    q_wait()
    inner_to_core(1)
    gather(1, q_recv[0] - update_sum(0))
    spread_y(0, reach[0])
    inner_wait(1)
    early = apply_inner(1, solved)
    solved = solve(1)

    update_to_x(1, early + apply_inner(2, solved))
    spread_z(1, reach[1])
    gather(2, q_recv[1] - update_sum(1))
    spread_y(1, reach[1])
    solve(2)
    spread_z(2, reach[2])
    spread_y(2, reach[2])

    spread_done(0, reach[0])
    spread_done(1, reach[1])
    wait_bytes(first_send.at[pl.ds(0, X * Z - 1)], first_ssem.at[0])
    wait_bytes(p_send.at[:, pl.ds(0, X - 1)], p_ssem.at[0])
    wait_bytes(q_send.at[:, pl.ds(0, Z - 1)], q_ssem.at[0])
    for slot in range(2):
        block = inner_v.at[steps[slot], pl.ds(1, Z - 1), my_half]
        wait_bytes(block, l_ssem.at[slot])
        wait_bytes(block, h_ssem.at[slot])
        wait_bytes(u_send.at[slot, pl.ds(0, X - 1)], u_ssem.at[slot])
    for k in range(3):
        gather_done(k)
    spread_done(2, reach[2])


def on_device(sizes, lower_prev, inner_blocks, diag_inverse, known_rows, right_sides):
    X, Y, Z = sizes
    step_rows = X * Y * Z * T
    f32 = jnp.float32
    dma = pltpu.SemaphoreType.DMA
    return pl.pallas_call(
        functools.partial(kernel, sizes),
        out_shape=pltpu.VMEM((3, step_rows // X, Z * LANES), f32),
        in_specs=[pl.BlockSpec(memory_space=pl.ANY)] * 5,
        out_specs=pl.BlockSpec(memory_space=pltpu.VMEM),
        scratch_shapes=[
            pltpu.VMEM(lower_prev.shape, f32),
            pltpu.VMEM(known_rows.shape, f32),
            pltpu.VMEM(diag_inverse.shape, f32),
            pltpu.VMEM(diag_inverse.shape, jnp.bfloat16),
            pltpu.VMEM(diag_inverse.shape, jnp.bfloat16),
            pltpu.VMEM(right_sides.shape, f32),
            pltpu.VMEM((3, Z) + inner_blocks.shape[1:], f32),
            pltpu.VMEM((X * Z, T, LANES), f32),
            pltpu.VMEM((X * Z, T, LANES), f32),
            pltpu.VMEM((2, X, T, Z * LANES), f32),
            pltpu.VMEM((2, X, T, Z * LANES), f32),
            pltpu.VMEM((2, Z, T, LANES), f32),
            pltpu.VMEM((2, Z, T, LANES), f32),
            pltpu.VMEM((3, Z, T, LANES), f32),
            pltpu.VMEM((3, Y, Z, X, T, LANES), f32),
            pltpu.VMEM((2, X, Z, T, LANES), f32),
            pltpu.VMEM((2, X, Z, T, LANES), f32),
            dma((4,)),
            dma((max(1, Z // 2),)),
            dma((1,)), dma((1,)),
            dma((1,)), dma((1,)),
            dma((1,)), dma((1,)),
            dma((2,)), dma((2,)),
            dma((2,)), dma((2,)),
            dma((2,)), dma((2,)),
            dma((3, X * Y)), dma((3, X * Y)),
            dma((3, Z)), dma((3, Z)),
            dma((3,)), dma((3,)),
        ],
        compiler_params=pltpu.CompilerParams(
            collective_id=0, has_side_effects=True, vmem_limit_bytes=56 * 1024 * 1024
        ),
    )(lower_prev, inner_blocks, diag_inverse, known_rows, right_sides)


def solution(mesh):
    X = mesh.shape["depth"]
    Y = 4 if mesh.shape["row"] == 32 else 2
    sizes = (X, Y, mesh.shape["row"] // Y)
    placed = (
        P(None, "row", "depth"),
        P(None, "row", "depth"),
        P(None, "depth", None),
        P("depth", "col"),
        P(None, "row", "col"),
    )
    return jax.shard_map(
        functools.partial(on_device, sizes),
        mesh=mesh,
        in_specs=placed,
        out_specs=P(None, "depth", "col"),
        check_vma=False,
    )
```

time: 71.3 us -> 62.8 us (0.88)
  Pallas kernels: 69.2 us -> 60.1 us
    pallas_call x1, Pallas kernels: 69.2 us -> 60.1 us  [on_device(): pl.pallas_call(functools.partial(kernel, sizes), out_shape=pltpu.VMEM((3,...]
where the time goes in v3:
time: 62.8 us; the launch traced here: 61.8 us
  Pallas kernels  60.1 us (96%)
  local copies, waits for them, and re-layouts  1.67 us (3%)
    pallas_call x1, Pallas kernels, on_device(): pl.pallas_call(functools.partial(kernel, sizes), out_shape=pltpu.VMEM((3,...  60.1 us
    unnamed x1, local copies, waits for them, and re-layouts  1.67 us

profile of v3, /device:TPU:2, one launch (start us, length us, event | category | flops | bytes accessed | tf_op | source)
XLA Modules:
  0.0 61.8 jit_solution(7991891738882697325)
XLA Ops:
  0.0 60.1 %shard_map.55 = f32[3,256,1024]{2,1,0:T(8,128)S(1)} custom-call(f32[3,32,1024]{2,1,0:T(8,128)} %lower_hbm.1, f32[3,32,256]{2,1,0:T(8,128)} %inner_hbm.1, f32[3,256,1024]{2,1,0:T(8,128)} %inverse_hbm.1, f32[1024,1024]{1,0:T(8,128)} %known_hbm.1, f32[3,32,1024]{2,1,0:T(8,128)} %right_hbm.1), custom_call_target="tpu_custom_call" | custom-call | tf_op jit(solution)/shard_map/pallas_call | solution.py:346
  60.1 1.7 %copy.7 = f32[3,256,1024]{2,1,0:T(8,128)} copy(f32[3,256,1024]{2,1,0:T(8,128)S(1)} %shard_map.55) | data formatting | bytes 6291456

commit v4 on v3

--- a/solution.py
+++ b/solution.py
@@ -29,6 +29,10 @@
     return both[:, :width] + (both[:, width:] + dot(a_low, b_high))
 
 
+def wrap(value, extent):
+    return jnp.where(value >= extent, value - extent, value)
+
+
 def wait_bytes(ref, sem):
     pltpu.make_async_copy(ref, ref, sem).wait()
 
@@ -38,7 +42,7 @@
     lower_hbm, inner_hbm, inverse_hbm, known_hbm, right_hbm,
     out_ref,
     lower_v, known_v, inverse_v, inverse_high, inverse_low, right_v, inner_v,
-    first_send, first_recv, p_send, p_recv, q_send, q_recv, acc_v, red_v, u_send, u_recv,
+    first_send, first_recv, p_send, p_recv, q_send, q_recv, acc_v, red_v, product_v, u_send, u_recv,
     in_sem, known_sem,
     first_ssem, first_rsem, p_ssem, p_rsem, q_ssem, q_rsem, l_ssem, l_rsem, h_ssem, h_rsem, u_ssem, u_rsem, g_ssem, g_rsem,
     a_ssem, a_rsem, b_ssem, b_rsem,
@@ -57,13 +61,13 @@
     width = Z * LANES // n_chunks
 
     def on_x(o):
-        return (row, col, lax.rem(x + o, X))
+        return (row, col, wrap(x + o, X))
 
     def on_y(o):
-        return (lax.rem(y + o, Y) * Z + z, col, x)
+        return (wrap(y + o, Y) * Z + z, col, x)
 
     def on_z(o):
-        return (y * Z + lax.rem(z + o, Z), col, x)
+        return (y * Z + wrap(z + o, Z), col, x)
 
     def z_lanes(pz):
         return pl.ds(pl.multiple_of(pz * LANES, LANES), LANES)
@@ -87,16 +91,6 @@
         ((dx, dy) for dx in range(X) for dy in range(Y) if dx or dy),
         key=lambda d: -(far(d[0], X) + far(d[1], Y)),
     )
-
-    barrier = pltpu.get_barrier_semaphore()
-    for dx, dz in xz:
-        device = (y * Z + lax.rem(z + dz, Z), col, lax.rem(x + dx, X))
-        pl.semaphore_signal(barrier, inc=1, device_id=device, device_id_type=MESH)
-    for o in range(1, Y):
-        pl.semaphore_signal(barrier, inc=1, device_id=on_y(o), device_id_type=MESH)
-
-    other_core = (row, 1 - col, x)
-    pl.semaphore_signal(barrier, inc=1, device_id=other_core, device_id_type=MESH)
 
     lower_in = pltpu.make_async_copy(lower_hbm, lower_v, in_sem.at[0])
     lower_in.start()
@@ -112,6 +106,16 @@
     inner_in.start()
     inverse_in = pltpu.make_async_copy(inverse_hbm, inverse_v, in_sem.at[3])
     inverse_in.start()
+
+    barrier = pltpu.get_barrier_semaphore()
+    for dx, dz in xz:
+        device = (y * Z + wrap(z + dz, Z), col, wrap(x + dx, X))
+        pl.semaphore_signal(barrier, inc=1, device_id=device, device_id_type=MESH)
+    for o in range(1, Y):
+        pl.semaphore_signal(barrier, inc=1, device_id=on_y(o), device_id_type=MESH)
+
+    other_core = (row, 1 - col, x)
+    pl.semaphore_signal(barrier, inc=1, device_id=other_core, device_id_type=MESH)
 
     for yy in range(1, Y):
         @pl.when(yy > x)
@@ -153,8 +157,8 @@
 
     def first_to_xz():
         for dx, dz in xz:
-            xd = lax.rem(x + dx, X)
-            zd = lax.rem(z + dz, Z)
+            xd = wrap(x + dx, X)
+            zd = wrap(z + dz, Z)
             send(
                 first_send.at[xd * Z + zd], first_recv.at[me],
                 first_ssem.at[0], first_rsem.at[0], (y * Z + zd, col, xd),
@@ -170,7 +174,7 @@
 
     def p_to_x():
         for o in far_first(X):
-            there = lax.rem(x + o, X)
+            there = wrap(x + o, X)
             send(p_send.at[:, there], p_recv.at[:, o], p_ssem.at[0], p_rsem.at[0], on_x(o))
 
     def p_to_z():
@@ -183,7 +187,7 @@
                 q_send[k, zd] = total[:, zd * LANES : (zd + 1) * LANES]
             q_recv[k, z] = q_send[k, z]
         for o in far_first(Z):
-            there = lax.rem(z + o, Z)
+            there = wrap(z + o, Z)
             send(q_send.at[:, there], q_recv.at[:, z], q_ssem.at[0], q_rsem.at[0], on_z(o))
 
     def q_wait():
@@ -211,35 +215,43 @@
         acc_v[k] = value
         red_v[k, y, :, x] = value
         for i, (dx, dy) in enumerate(xy):
-            xd = lax.rem(x + dx, X)
+            xd = wrap(x + dx, X)
 
             @pl.when(xd >= y)
             def _():
                 send(
                     acc_v.at[k], red_v.at[k, y, :, x], g_ssem.at[k, i], g_rsem.at[k, i],
-                    (lax.rem(y + dy, Y) * Z + z, col, xd),
+                    (wrap(y + dy, Y) * Z + z, col, xd),
                 )
-
-    def gather_wait(k):
-        for i, (dx, dy) in enumerate(xy):
-            ys = lax.rem(y + Y - dy, Y)
-
-            @pl.when(ys <= x)
-            def _():
-                wait_bytes(red_v.at[k, ys, :, lax.rem(x + X - dx, X)], g_rsem.at[k, i])
 
     def gather_done(k):
         for i, (dx, dy) in enumerate(xy):
 
-            @pl.when(lax.rem(x + dx, X) >= y)
+            @pl.when(wrap(x + dx, X) >= y)
             def _():
                 wait_bytes(acc_v.at[k], g_ssem.at[k, i])
 
     def solve(k):
-        gather_wait(k)
-        value = three_pass(
-            inverse_high[k], inverse_low[k], red_v[k].reshape(step_rows, LANES)
-        )
+        part = Z * X * T
+        for dy in (0, *far_first(Y)[::-1]):
+            ys = wrap(y + Y - dy, Y)
+            for i, d in enumerate(xy):
+                if d[1] == dy:
+
+                    @pl.when(ys <= x)
+                    def _():
+                        xs = wrap(x + X - d[0], X)
+                        wait_bytes(red_v.at[k, ys, :, xs], g_rsem.at[k, i])
+
+            columns = pl.ds(pl.multiple_of(ys * part, part), part)
+            product_v[ys] = three_pass(
+                inverse_high[k, :, columns],
+                inverse_low[k, :, columns],
+                red_v[k, ys].reshape(part, LANES),
+            )
+        value = product_v[0]
+        for ys in range(1, Y):
+            value = value + product_v[ys]
         out_ref[k, :, z_lanes(z)] = value
         return value
 
@@ -249,9 +261,9 @@
 
     def update_to_x(j, value):
         for o in range(Z):
-            u_send[j, :, lax.rem(z + Z - o, Z)] = value[o]
+            u_send[j, :, wrap(z + Z - o, Z)] = value[o]
         for o in far_first(X):
-            there = lax.rem(x + o, X)
+            there = wrap(x + o, X)
             send(u_send.at[j, there], u_recv.at[j, o], u_ssem.at[j], u_rsem.at[j], on_x(o))
 
     def update_sum(j):
@@ -276,7 +288,7 @@
     def spread_y(k, reach):
         for o in far_first(Z)[::-1]:
             if far(o, Z) > reach:
-                block = out_ref.at[k, own_rows, z_lanes(lax.rem(z + Z - o, Z))]
+                block = out_ref.at[k, own_rows, z_lanes(wrap(z + Z - o, Z))]
                 wait_bytes(block, a_rsem.at[k, o])
                 for p in far_first(Y):
                     send(block, block, b_ssem.at[k], b_rsem.at[k], on_y(p))
@@ -364,6 +376,7 @@
             pltpu.VMEM((2, Z, T, LANES), f32),
             pltpu.VMEM((3, Z, T, LANES), f32),
             pltpu.VMEM((3, Y, Z, X, T, LANES), f32),
+            pltpu.VMEM((Y, step_rows // X, LANES), f32),
             pltpu.VMEM((2, X, Z, T, LANES), f32),
             pltpu.VMEM((2, X, Z, T, LANES), f32),
             dma((4,)),

time: 62.8 us -> 62.2 us (level); the launches traced: 61.8 us -> 62 us
  no operation moved by 1% of the time
where the time goes in v4:
time: 62.2 us; the launch traced here: 62 us
  Pallas kernels  60.3 us (97%)
  local copies, waits for them, and re-layouts  1.67 us (3%)
    pallas_call x1, Pallas kernels, on_device(): pl.pallas_call(functools.partial(kernel, sizes), out_shape=pltpu.VMEM((3,...  60.3 us
    unnamed x1, local copies, waits for them, and re-layouts  1.67 us

profile of v4, /device:TPU:2, one launch (start us, length us, event | category | flops | bytes accessed | tf_op | source)
XLA Modules:
  0.0 62.0 jit_solution(13437402342238231118)
XLA Ops:
  0.0 60.3 %shard_map.55 = f32[3,256,1024]{2,1,0:T(8,128)S(1)} custom-call(f32[3,32,1024]{2,1,0:T(8,128)} %lower_hbm.1, f32[3,32,256]{2,1,0:T(8,128)} %inner_hbm.1, f32[3,256,1024]{2,1,0:T(8,128)} %inverse_hbm.1, f32[1024,1024]{1,0:T(8,128)} %known_hbm.1, f32[3,32,1024]{2,1,0:T(8,128)} %right_hbm.1), custom_call_target="tpu_custom_call" | custom-call | tf_op jit(solution)/shard_map/pallas_call | solution.py:358
  60.3 1.7 %copy.7 = f32[3,256,1024]{2,1,0:T(8,128)} copy(f32[3,256,1024]{2,1,0:T(8,128)S(1)} %shard_map.55) | data formatting | bytes 6291456

commit v5 on v4

--- a/solution.py
+++ b/solution.py
@@ -87,11 +87,6 @@
         ((dx, dz) for dx in range(X) for dz in range(Z) if dx or dz),
         key=lambda d: -(far(d[0], X) + far(d[1], Z)),
     )
-    xy = sorted(
-        ((dx, dy) for dx in range(X) for dy in range(Y) if dx or dy),
-        key=lambda d: -(far(d[0], X) + far(d[1], Y)),
-    )
-
     lower_in = pltpu.make_async_copy(lower_hbm, lower_v, in_sem.at[0])
     lower_in.start()
     known_in = []
@@ -211,37 +206,40 @@
     def inner_wait(slot):
         wait_bytes(inner_v.at[steps[slot], pl.ds(1, Z - 1), my_half], h_rsem.at[slot])
 
+    order = [(xd, dy) for xd in range(X - 1, -1, -1) for dy in far_first(Y) + [0]]
+
+    def sends(xd, dy):
+        return (xd >= y) & (xd != x) if dy == 0 else xd >= y
+
     def gather(k, value):
         acc_v[k] = value
         red_v[k, y, :, x] = value
-        for i, (dx, dy) in enumerate(xy):
-            xd = wrap(x + dx, X)
-
-            @pl.when(xd >= y)
+        for xd, dy in order:
+
+            @pl.when(sends(xd, dy))
             def _():
                 send(
-                    acc_v.at[k], red_v.at[k, y, :, x], g_ssem.at[k, i], g_rsem.at[k, i],
+                    acc_v.at[k], red_v.at[k, y, :, x],
+                    g_ssem.at[k, xd * Y + dy], g_rsem.at[k, x * Y + dy],
                     (wrap(y + dy, Y) * Z + z, col, xd),
                 )
 
     def gather_done(k):
-        for i, (dx, dy) in enumerate(xy):
-
-            @pl.when(wrap(x + dx, X) >= y)
+        for xd, dy in order:
+
+            @pl.when(sends(xd, dy))
             def _():
-                wait_bytes(acc_v.at[k], g_ssem.at[k, i])
+                wait_bytes(acc_v.at[k], g_ssem.at[k, xd * Y + dy])
 
     def solve(k):
         part = Z * X * T
         for dy in (0, *far_first(Y)[::-1]):
             ys = wrap(y + Y - dy, Y)
-            for i, d in enumerate(xy):
-                if d[1] == dy:
-
-                    @pl.when(ys <= x)
-                    def _():
-                        xs = wrap(x + X - d[0], X)
-                        wait_bytes(red_v.at[k, ys, :, xs], g_rsem.at[k, i])
+            for xs in range(X):
+
+                @pl.when((ys <= x) & (xs != x) if dy == 0 else ys <= x)
+                def _():
+                    wait_bytes(red_v.at[k, ys, :, xs], g_rsem.at[k, xs * Y + dy])
 
             columns = pl.ds(pl.multiple_of(ys * part, part), part)
             product_v[ys] = three_pass(

time: 62.2 us -> 62 us (level)
  no operation moved by 1% of the time
where the time goes in v5:
time: 62 us; the launch traced here: 61.9 us
  Pallas kernels  60.2 us (97%)
  local copies, waits for them, and re-layouts  1.67 us (3%)
    pallas_call x1, Pallas kernels, on_device(): pl.pallas_call(functools.partial(kernel, sizes), out_shape=pltpu.VMEM((3,...  60.2 us
    unnamed x1, local copies, waits for them, and re-layouts  1.67 us

profile of v5, /device:TPU:2, one launch (start us, length us, event | category | flops | bytes accessed | tf_op | source)
XLA Modules:
  0.0 61.9 jit_solution(11053766657427486715)
XLA Ops:
  0.0 60.2 %shard_map.55 = f32[3,256,1024]{2,1,0:T(8,128)S(1)} custom-call(f32[3,32,1024]{2,1,0:T(8,128)} %lower_hbm.1, f32[3,32,256]{2,1,0:T(8,128)} %inner_hbm.1, f32[3,256,1024]{2,1,0:T(8,128)} %inverse_hbm.1, f32[1024,1024]{1,0:T(8,128)} %known_hbm.1, f32[3,32,1024]{2,1,0:T(8,128)} %right_hbm.1), custom_call_target="tpu_custom_call" | custom-call | tf_op jit(solution)/shard_map/pallas_call | solution.py:356
  60.2 1.7 %copy.7 = f32[3,256,1024]{2,1,0:T(8,128)} copy(f32[3,256,1024]{2,1,0:T(8,128)S(1)} %shard_map.55) | data formatting | bytes 6291456
